TPU v7x, 128 devices: a whole 4x4x4 slice. The times are simulated.
128 devices in a mesh: grp: 4 (over y), dev: 32 (over z, x, core).
Axes of the slice: x: 4, y: 4, z: 4, core: 2. Of those that a mesh axis runs over, the one named last changes fastest.
Arguments:
- points: float32 [64, 196608], P(None, 'dev'), may hold values from -6 to 6
- weights: float32 [196608, 128], P('dev'), may hold values from -4 to 4
- proj: float32 [256, 196608], P(None, 'dev'), may hold values from -0.078125 to 0.078125
- fetch_table: int32 [3, 32, 32, 2], P(None, 'dev'), may hold values from 0 to 11, as said below
- near_list: int32 [384, 16], P('dev'), may hold values from 0 to 63, as said below
- far_list: int32 [384, 8], P('dev'), may hold values from 0 to 31, as said below
- skel_idx: int32 [32, 256], P('dev'), may hold values from 0 to 6143, as said below
Outputs:
- potential: float32 [196608, 128], P('dev')
Inputs may be any that keep to these rules, and one draw needn't show every extreme that they name: Entries of fetch_table[r, d, e] are distinct local leaf numbers of column e. `near_list`: the 16 slots of one target leaf are distinct. `far_list`: the 8 nodes of one target leaf are distinct, and one of them is node (c + 1) mod 32 for the leaf's column c. `skel_idx`: the 256 skeleton points of one node are distinct.
All inputs are finite; a program needn't handle non-finite values.
Results may differ from a plain program's by a relative error of at most 0.0003.
Values sent between devices are 32-bit elements; how exact they have to be, the bound alone decides.
A program may use at most 192 MiB of HBM per device.

v0:
```python
import jax
import jax.numpy as jnp
from jax import lax
from jax.sharding import PartitionSpec as P


def kernel_sum(target, sources, values):
    high = lax.Precision.HIGHEST
    inner = jnp.einsum("dt,jds->tjs", target, sources, precision=high)
    target_norm = jnp.sum(target * target, axis=0)
    source_norm = jnp.sum(sources * sources, axis=1)
    distance = target_norm[:, None, None] + source_norm[None] - 2.0 * inner
    kernel = jnp.exp(-distance * (2.0 / target.shape[0]))
    return jnp.einsum("tjs,jsw->tw", kernel, values, precision=high)


def on_device(points, weights, proj, fetch_table, near_list, far_list, skel_idx):
    features, column_points = points.shape
    columns = weights.shape[1]
    devices = lax.axis_size("dev")
    groups = lax.axis_size("grp")
    targets = near_list.shape[0]
    leaf_size = column_points // targets
    row_leaves = targets // (groups - 1)
    capacity = fetch_table.shape[3]
    skeleton = skel_idx.shape[1]
    group_index = lax.axis_index("grp")
    near_row = jnp.minimum(group_index, groups - 2)
    far_side = group_index == groups - 1
    leaf_coords = points.reshape(features, targets, leaf_size)
    leaf_weights = weights.reshape(targets, leaf_size, columns)
    requests = lax.dynamic_index_in_dim(fetch_table[:, 0], near_row, 0, keepdims=False)
    asked = lax.all_to_all(requests, "dev", split_axis=0, concat_axis=0, tiled=True)
    coords = jnp.moveaxis(jnp.take(leaf_coords, asked, axis=1), 0, 2)
    values = jnp.take(leaf_weights, asked, axis=0)
    fetched_coords = lax.all_to_all(coords, "dev", split_axis=0, concat_axis=0, tiled=True)
    fetched_values = lax.all_to_all(values, "dev", split_axis=0, concat_axis=0, tiled=True)
    flat_coords = fetched_coords.reshape(devices * capacity, features, leaf_size)
    flat_values = fetched_values.reshape(devices * capacity, leaf_size, columns)
    local_skeleton = jnp.take(points, skel_idx[0], axis=1)
    share_len = column_points // groups
    share_start = group_index * share_len
    share_proj = lax.dynamic_slice_in_dim(proj, share_start, share_len, 1)
    share_weights = lax.dynamic_slice_in_dim(weights, share_start, share_len, 0)
    partial_value = jnp.dot(
        share_proj,
        share_weights,
        preferred_element_type=jnp.float32,
        precision=lax.Precision.HIGHEST,
    )
    node_index = lax.axis_index("dev")
    owner_mask = jnp.where(far_side, 1.0, 0.0).astype(jnp.float32)
    table_coords = jnp.zeros((devices, features, skeleton), jnp.float32)
    table_coords = lax.dynamic_update_index_in_dim(
        table_coords, local_skeleton * owner_mask, node_index, 0
    )
    table_weights = jnp.zeros((devices, skeleton, columns), jnp.float32)
    table_weights = lax.dynamic_update_index_in_dim(table_weights, partial_value, node_index, 0)
    skel_coords, skel_weights = lax.psum((table_coords, table_weights), ("grp", "dev"))

    def near_work():
        slots = lax.dynamic_slice_in_dim(near_list, near_row * row_leaves, row_leaves, 0)
        leaf_numbers = near_row * row_leaves + jnp.arange(row_leaves, dtype=jnp.int32)

        def near_leaf(items):
            leaf_number, leaf_slots = items
            target = jnp.take(leaf_coords, leaf_number, axis=1)
            return kernel_sum(
                target,
                jnp.take(flat_coords, leaf_slots, axis=0),
                jnp.take(flat_values, leaf_slots, axis=0),
            )

        block = lax.map(near_leaf, (leaf_numbers, slots))
        empty = jnp.zeros((targets, leaf_size, columns), jnp.float32)
        return lax.dynamic_update_slice_in_dim(empty, block, near_row * row_leaves, 0)

    def far_work():

        def far_leaf(items):
            leaf_number, node_ids = items
            target = jnp.take(leaf_coords, leaf_number, axis=1)
            return kernel_sum(
                target,
                jnp.take(skel_coords, node_ids, axis=0),
                jnp.take(skel_weights, node_ids, axis=0),
            )

        return lax.map(far_leaf, (jnp.arange(targets, dtype=jnp.int32), far_list))

    contribution = lax.cond(far_side, far_work, near_work)
    total = lax.psum(contribution, "grp")
    return total.reshape(column_points, columns)


def solution(mesh):
    placed = (
        P(None, "dev"),
        P("dev", None),
        P(None, "dev"),
        P(None, "dev", None, None),
        P("dev", None),
        P("dev", None),
        P("dev", None),
    )
    return jax.shard_map(
        on_device, mesh=mesh, in_specs=placed, out_specs=P("dev", None), check_vma=False
    )
```

profile of v0, /device:TPU:1, one launch (start us, length us, event | category | flops | bytes accessed | tf_op | source)
XLA Modules:
  0.0 820.4 jit_solution(13350892789192930071)
XLA Ops:
  6.5 0.8 fusion.82
  7.4 0.7 copy.36
  8.1 9.4 %all-to-all-start = ((s32[32,1,2]{2,1,0:T(1,128)}), s32[32,1,2]{2,1,0:T(1,128)S(1)}, u32[]{:S(2)}, u32[]{:S(2)}) async-start(s32[32,1,2]{2,1,0:T(1,128)} %copy.36), calls=%async_computation | async-start | bytes 32768 | tf_op jit(solution)/shard_map/all_to_all | solution.py:33
  17.5 2.7 copy.64
  20.2 4.2 all-to-all-done
  24.4 0.1 copy.37
  24.5 0.1 copy.40
  24.6 0.1 reshape.285
  24.7 0.1 copy.38
  24.8 5.7 gather_fusion.4
  30.6 8.5 %broadcast_select_fusion.1 = f32[32,2,64,512]{3,2,1,0:T(8,128)} fusion(f32[32,2,64,512]{3,2,1,0:T(8,128)} %bitcast.103, pred[32,2]{1,0:T(8,128)(4,1)S(1)} %copy.38), kind=kLoop, calls=%fused_computation.87 | loop fusion | flops 2097152 | bytes 16777280 | tf_op jit(solution)/shard_map/jit(_take)/select_n | solution.py:34
  39.1 5.2 all-to-all-start.1
  44.3 7.4 gather_fusion.5
  51.6 11.6 %broadcast_select_fusion = f32[32,2,512,128]{3,2,1,0:T(8,128)} fusion(f32[32,2,512,128]{3,2,1,0:T(8,128)} %bitcast.101, pred[32,2]{1,0:T(8,128)(4,1)S(1)} %copy.38), kind=kLoop, calls=%fused_computation.86 | loop fusion | flops 4194304 | bytes 33554496 | tf_op jit(solution)/shard_map/jit(_take)/select_n | solution.py:35
  63.2 80.8 %all-to-all-done.1 = f32[32,2,64,512]{3,2,1,0:T(8,128)} async-done(((f32[32,2,64,512]{3,2,1,0:T(8,128)}), f32[32,2,64,512]{3,2,1,0:T(8,128)}, u32[]{:S(2)}, u32[]{:S(2)}) %all-to-all-start.1) | async-done | bytes 8388640 | tf_op jit(solution)/shard_map/all_to_all | solution.py:36
  144.0 11.3 %all-to-all-start.2 = ((f32[32,2,512,128]{3,2,1,0:T(8,128)}), f32[32,2,512,128]{3,2,1,0:T(8,128)}, u32[]{:S(2)}, u32[]{:S(2)}) async-start(f32[32,2,512,128]{3,2,1,0:T(8,128)} %broadcast_select_fusion), calls=%async_computation.2 | async-start | bytes 33554432 | tf_op jit(solution)/shard_map/all_to_all | solution.py:37
  155.3 0.0 all-reduce.6.cloned.1.call-start
  155.4 3.3 copy.43
  158.6 2.6 gather_fusion.6
  161.3 0.1 copy.44
  161.3 2.4 broadcast_in_dim.110
  163.8 3.5 fusion.75
  167.2 1.6 broadcast_in_dim.107
  168.8 0.6 fusion.80
  169.4 0.0 all-reduce.6.cloned.1.call-update
  169.5 0.0 all-reduce.4.cloned.1.call-start
  169.5 1.9 reshape.193
  171.4 310.3 %all-reduce.6.cloned.1.call-done = (f32[32,64,256]{2,1,0:T(8,128)}, f32[32,256,128]{2,1,0:T(8,128)}) async-done(((f32[32,64,256]{2,1,0:T(8,128)}, f32[32,256,128]{2,1,0:T(8,128)}), (f32[32,64,256]{2,1,0:T(8,128)}, f32[32,256,128]{2,1,0:T(8,128)})) %all-reduce.6.cloned.1.call-update) | async-done | bytes 6291472 | tf_op jit(solution)/shard_map/psum | solution.py:59
  481.8 223.2 %conditional.1 = (f32[12,512,128]{2,1,0:T(8,128)}) conditional(s32[]{:T(128)} %convert_element_type.3, (s32[]{:T(128)}, s32[12,16]{1,0:T(8,128)}, f32[32,2,64,512]{3,2,1,0:T(8,128)}, f32[32,2,512,128]{3,2,1,0:T(8,128)}, f32[64,12,512]{2,1,0:T(8,128)}) %tuple.20, (f32[64,12,512]{2,1,0:T(8,128)}, s32[12,8]{0,1:T(8,128)S(1)}, f32[32,64,256]{2,1,0:T(8,128)}, ...), branch_computations={%region_2.0_spmd, %region_7.13_spmd} | conditional | flops 9687917568 | bytes 60630836 | solution.py:91
  481.8 0.7 constant_dynamic-slice_fusion.2
  482.4 218.3 %while.19 = (s32[]{:T(128)}, f32[4,512,128]{2,1,0:T(8,128)}, s32[4]{0:T(128)S(1)}, f32[64,12,512]{2,1,0:T(8,128)}, s32[4,16]{1,0:T(4,128)S(1)}, /*index=5*/f32[6...) while((s32[]{:T(128)}, f32[4,512,128]{2,1,0:T(8,128)}, ...), condition=%wide.region_6.7_spmd, body=%wide.region_3.6_spmd.sunk | while | flops 9687917568 | bytes 55387260 | solution.py:74
  482.5 0.6 dynamic_slice.65
  484.9 1.3 constant_dynamic-slice_fusion.9
  486.3 4.1 gather_fusion.3
  490.4 16.2 %fusion.112 = f32[512,16,512]{2,0,1:T(8,128)} fusion(f32[16,64,512]{2,1,0:T(8,128)S(1)} %gather_fusion.3, pred[16]{0:T(512)(128)(4,1)S(1)} %compare_and_fusion.7, f32[64,1,512]{2,1,0:T(1,128)S(1)} %constant_dynamic-slice_fusion.9, pred[]{:T(512)S(6)} %and.57), kind=kOutput, calls=%fused_computation.22.clone.1 | convolution fusion | flops 3221782528 | bytes 19005456 | tf_op jit(solution)/shard_map/cond/branch_0_fun/while/body/eval_jaxpr/dt,jds->tjs/dot_general | solution.py:9
  506.6 0.4 multiply_reduce_fusion.5
  507.0 8.5 %gather_fusion.2 = f32[16,512,128]{2,1,0:T(8,128)} fusion(f32[64,512,128]{2,1,0:T(8,128)} %get-tuple-element.330, s32[1024]{0:T(1024)S(1)} %pad_clamp_fusion.7), kind=kCustom, calls=%fused_computation.1.clone.1 | custom fusion | bytes 8388672 | tf_op jit(solution)/shard_map/cond/branch_0_fun/while/body/eval_jaxpr/jit(_take)/gather | solution.py:71
  515.5 21.5 %fusion.114 = f32[4,512,128]{2,1,0:T(8,128)} fusion(f32[4,512,128]{2,1,0:T(8,128)} %get-tuple-element.314, s32[]{:T(128)} %get-tuple-element.313, f32[16,512,128]{2,1,0:T(8,128)} %gather_fusion.2, pred[16]{0:T(512)(128)(4,1)S(1)} %compare_and_fusion.7, f32[512,16,512]{2,0,1:T(8,128)} %fusion.112, f32[16,512]{1,0:T(8,128)S(1)} %multiply_reduce_fusion.5, ...), kind=kOutput, calls=%fused_computation.25.clone.1 | convolution fusion | flops 6464471040 | bytes 21269008 | tf_op jit(solution)/shard_map/cond/branch_0_fun/while/body/eval_jaxpr/tjs,jsw->tw/dot_general | solution.py:14
  537.0 0.6 dynamic_slice.65
  539.5 1.3 constant_dynamic-slice_fusion.9
  540.9 4.1 gather_fusion.3
  545.0 16.2 %fusion.112 = f32[512,16,512]{2,0,1:T(8,128)} fusion(f32[16,64,512]{2,1,0:T(8,128)S(1)} %gather_fusion.3, pred[16]{0:T(512)(128)(4,1)S(1)} %compare_and_fusion.7, f32[64,1,512]{2,1,0:T(1,128)S(1)} %constant_dynamic-slice_fusion.9, pred[]{:T(512)S(6)} %and.57), kind=kOutput, calls=%fused_computation.22.clone.1 | convolution fusion | flops 3221782528 | bytes 19005456 | tf_op jit(solution)/shard_map/cond/branch_0_fun/while/body/eval_jaxpr/dt,jds->tjs/dot_general | solution.py:9
  561.2 0.4 multiply_reduce_fusion.5
  561.5 8.5 %gather_fusion.2 = f32[16,512,128]{2,1,0:T(8,128)} fusion(f32[64,512,128]{2,1,0:T(8,128)} %get-tuple-element.330, s32[1024]{0:T(1024)S(1)} %pad_clamp_fusion.7), kind=kCustom, calls=%fused_computation.1.clone.1 | custom fusion | bytes 8388672 | tf_op jit(solution)/shard_map/cond/branch_0_fun/while/body/eval_jaxpr/jit(_take)/gather | solution.py:71
  570.1 21.5 %fusion.114 = f32[4,512,128]{2,1,0:T(8,128)} fusion(f32[4,512,128]{2,1,0:T(8,128)} %get-tuple-element.314, s32[]{:T(128)} %get-tuple-element.313, f32[16,512,128]{2,1,0:T(8,128)} %gather_fusion.2, pred[16]{0:T(512)(128)(4,1)S(1)} %compare_and_fusion.7, f32[512,16,512]{2,0,1:T(8,128)} %fusion.112, f32[16,512]{1,0:T(8,128)S(1)} %multiply_reduce_fusion.5, ...), kind=kOutput, calls=%fused_computation.25.clone.1 | convolution fusion | flops 6464471040 | bytes 21269008 | tf_op jit(solution)/shard_map/cond/branch_0_fun/while/body/eval_jaxpr/tjs,jsw->tw/dot_general | solution.py:14
  591.6 0.6 dynamic_slice.65
  594.1 1.3 constant_dynamic-slice_fusion.9
  595.4 4.1 gather_fusion.3
  599.5 16.2 %fusion.112 = f32[512,16,512]{2,0,1:T(8,128)} fusion(f32[16,64,512]{2,1,0:T(8,128)S(1)} %gather_fusion.3, pred[16]{0:T(512)(128)(4,1)S(1)} %compare_and_fusion.7, f32[64,1,512]{2,1,0:T(1,128)S(1)} %constant_dynamic-slice_fusion.9, pred[]{:T(512)S(6)} %and.57), kind=kOutput, calls=%fused_computation.22.clone.1 | convolution fusion | flops 3221782528 | bytes 19005456 | tf_op jit(solution)/shard_map/cond/branch_0_fun/while/body/eval_jaxpr/dt,jds->tjs/dot_general | solution.py:9
  615.7 0.4 multiply_reduce_fusion.5
  616.1 8.5 %gather_fusion.2 = f32[16,512,128]{2,1,0:T(8,128)} fusion(f32[64,512,128]{2,1,0:T(8,128)} %get-tuple-element.330, s32[1024]{0:T(1024)S(1)} %pad_clamp_fusion.7), kind=kCustom, calls=%fused_computation.1.clone.1 | custom fusion | bytes 8388672 | tf_op jit(solution)/shard_map/cond/branch_0_fun/while/body/eval_jaxpr/jit(_take)/gather | solution.py:71
  624.6 21.5 %fusion.114 = f32[4,512,128]{2,1,0:T(8,128)} fusion(f32[4,512,128]{2,1,0:T(8,128)} %get-tuple-element.314, s32[]{:T(128)} %get-tuple-element.313, f32[16,512,128]{2,1,0:T(8,128)} %gather_fusion.2, pred[16]{0:T(512)(128)(4,1)S(1)} %compare_and_fusion.7, f32[512,16,512]{2,0,1:T(8,128)} %fusion.112, f32[16,512]{1,0:T(8,128)S(1)} %multiply_reduce_fusion.5, ...), kind=kOutput, calls=%fused_computation.25.clone.1 | convolution fusion | flops 6464471040 | bytes 21269008 | tf_op jit(solution)/shard_map/cond/branch_0_fun/while/body/eval_jaxpr/tjs,jsw->tw/dot_general | solution.py:14
  646.2 0.6 dynamic_slice.65
  648.6 1.3 constant_dynamic-slice_fusion.9
  650.0 4.1 gather_fusion.3
  654.1 16.2 %fusion.112 = f32[512,16,512]{2,0,1:T(8,128)} fusion(f32[16,64,512]{2,1,0:T(8,128)S(1)} %gather_fusion.3, pred[16]{0:T(512)(128)(4,1)S(1)} %compare_and_fusion.7, f32[64,1,512]{2,1,0:T(1,128)S(1)} %constant_dynamic-slice_fusion.9, pred[]{:T(512)S(6)} %and.57), kind=kOutput, calls=%fused_computation.22.clone.1 | convolution fusion | flops 3221782528 | bytes 19005456 | tf_op jit(solution)/shard_map/cond/branch_0_fun/while/body/eval_jaxpr/dt,jds->tjs/dot_general | solution.py:9
  670.3 0.4 multiply_reduce_fusion.5
  670.7 8.5 %gather_fusion.2 = f32[16,512,128]{2,1,0:T(8,128)} fusion(f32[64,512,128]{2,1,0:T(8,128)} %get-tuple-element.330, s32[1024]{0:T(1024)S(1)} %pad_clamp_fusion.7), kind=kCustom, calls=%fused_computation.1.clone.1 | custom fusion | bytes 8388672 | tf_op jit(solution)/shard_map/cond/branch_0_fun/while/body/eval_jaxpr/jit(_take)/gather | solution.py:71
  679.2 21.5 %fusion.114 = f32[4,512,128]{2,1,0:T(8,128)} fusion(f32[4,512,128]{2,1,0:T(8,128)} %get-tuple-element.314, s32[]{:T(128)} %get-tuple-element.313, f32[16,512,128]{2,1,0:T(8,128)} %gather_fusion.2, pred[16]{0:T(512)(128)(4,1)S(1)} %compare_and_fusion.7, f32[512,16,512]{2,0,1:T(8,128)} %fusion.112, f32[16,512]{1,0:T(8,128)S(1)} %multiply_reduce_fusion.5, ...), kind=kOutput, calls=%fused_computation.25.clone.1 | convolution fusion | flops 6464471040 | bytes 21269008 | tf_op jit(solution)/shard_map/cond/branch_0_fun/while/body/eval_jaxpr/tjs,jsw->tw/dot_general | solution.py:14
  700.7 2.0 broadcast.190
  702.7 2.3 constant_dynamic-update-slice_fusion
  705.0 0.0 all-reduce.4.cloned.1.call-update
  705.0 104.8 %all-reduce.4.cloned.1.call-done = f32[6144,128]{1,0:T(8,128)} async-done(((f32[6144,128]{1,0:T(8,128)}), f32[6144,128]{1,0:T(8,128)}) %all-reduce.4.cloned.1.call-update) | async-done | bytes 3145744 | tf_op jit(solution)/shard_map/psum | solution.py:92
  809.8 3.8 copy.95
  (35 shorter events, 0.3 us)
Async XLA Ops:
  6.5 37.7 %copy-start = (f32[6144,128]{1,0:T(8,128)S(1)}, f32[6144,128]{1,0:T(8,128)}, u32[]{:S(2)}) copy-start(f32[6144,128]{1,0:T(8,128)} %param.16) | copy-start | bytes 9437188
  8.1 16.4 %all-to-all-start = ((s32[32,1,2]{2,1,0:T(1,128)}), s32[32,1,2]{2,1,0:T(1,128)S(1)}, u32[]{:S(2)}, u32[]{:S(2)}) async-start(s32[32,1,2]{2,1,0:T(1,128)} %copy.36), calls=%async_computation | async-start | bytes 32768 | tf_op jit(solution)/shard_map/all_to_all | solution.py:33
  39.1 105.0 %all-to-all-start.1 = ((f32[32,2,64,512]{3,2,1,0:T(8,128)}), f32[32,2,64,512]{3,2,1,0:T(8,128)}, u32[]{:S(2)}, u32[]{:S(2)}) async-start(f32[32,2,64,512]{3,2,1,0:T(8,128)} %broadcast_select_fusion.1), calls=%async_computation.1 | async-start | bytes 16777216 | tf_op jit(solution)/shard_map/all_to_all | solution.py:36
  144.0 337.7 %all-to-all-start.2 = ((f32[32,2,512,128]{3,2,1,0:T(8,128)}), f32[32,2,512,128]{3,2,1,0:T(8,128)}, u32[]{:S(2)}, u32[]{:S(2)}) async-start(f32[32,2,512,128]{3,2,1,0:T(8,128)} %broadcast_select_fusion), calls=%async_computation.2 | async-start | bytes 33554432 | tf_op jit(solution)/shard_map/all_to_all | solution.py:37
  155.3 3.3 copy-start.4
  155.3 326.4 %all-reduce.6.cloned.1.call-start = ((), (), s32[]{:S(2)}) async-start(), calls=%async_computation.4 | async-start | bytes 12582912 | tf_op jit(solution)/shard_map/psum | solution.py:59
  167.2 2.3 copy-start.2
  169.4 312.3 %copy-start.3 = (s32[12,8]{0,1:T(8,128)S(1)}, s32[12,8]{0,1:T(8,128)}, u32[]{:S(2)}) copy-start(s32[12,8]{0,1:T(8,128)} %param.20) | copy-start | bytes 1156
  169.5 640.3 %all-reduce.4.cloned.1.call-start = ((), (), s32[]{:S(2)}) async-start(), calls=%async_computation.3 | async-start | bytes 6291456 | tf_op jit(solution)/shard_map/psum | solution.py:92
  705.0 108.6 %copy-start.1 = (f32[6144,128]{1,0:T(8,128)S(1)}, f32[6144,128]{1,0:T(8,128)}, u32[]{:S(2)}) copy-start(f32[6144,128]{1,0:T(8,128)} %param.16) | copy-start | bytes 9437188
Sparse Core Ops, SparseCore 0:
  169.6 312.1 all-reduce.5
  705.1 104.6 all-reduce.3
where the time goes:
time: 823 us; the launch traced here: 820 us
  waiting for transfers between devices  500 us (61%)
  matrix products  154 us (19%)
  local copies, waits for them, and re-layouts  96.2 us (12%)
  starting transfers between devices  26 us (3%)
  other arithmetic  22.5 us (3%)
  between operations  13.5 us (2%)
    psum x1, waiting for transfers between devices, on_device(): lax.psum((table_coords, table_weights), ('grp', 'dev'))  310 us
    psum x1, waiting for transfers between devices, on_device(): total = lax.psum(contribution, 'grp')  105 us
    dot_general x4, matrix products, kernel_sum(): return jnp.einsum('tjs,jsw->tw', kernel, values, precision=high)  86.1 us
    all_to_all x1, waiting for transfers between devices, on_device(): lax.all_to_all(coords, 'dev', split_axis=0, concat_axis=0, tiled=True)  80.8 us
    dot_general x4, matrix products, kernel_sum(): inner = jnp.einsum('dt,jds->tjs', target, sources, precision=high)  64.7 us
    gather x4, local copies, waits for them, and re-layouts, near_leaf(): jnp.take(flat_values, leaf_slots, axis=0)  34 us
  transfers between devices with their start and end apart: 5, of which 4 were waited for; matrix products, arithmetic and copies ran while one was open for 5% of the time, Pallas kernels for 0%

commit v1 on v0

--- a/solution.py
+++ b/solution.py
@@ -89,7 +89,7 @@
         return lax.map(far_leaf, (jnp.arange(targets, dtype=jnp.int32), far_list))
 
     contribution = lax.cond(far_side, far_work, near_work)
-    total = lax.psum(contribution, "grp")
+    total = jnp.sum(lax.all_gather(contribution, "grp"), axis=0)
     return total.reshape(column_points, columns)
 
 

time: 823 us -> 870 us (1.057)
  waiting for transfers between devices: 500 us -> 543 us
    all_gather x0 -> x1, waiting for transfers between devices: none -> 148 us  [on_device(): total = jnp.sum(lax.all_gather(contribution, 'grp'), axis=0)]
    psum x1 -> x0, waiting for transfers between devices: 105 us -> none  [on_device(): total = lax.psum(contribution, 'grp')]
  transfers between devices with their start and end apart: 5 -> 5, of which waited for: 4 -> 4; matrix products, arithmetic and copies ran while one was open for 5% -> 4% of each run, Pallas kernels for 0% -> 0%
where the time goes in v1:
time: 870 us; the launch traced here: 867 us
  waiting for transfers between devices  543 us (62%)
  matrix products  154 us (18%)
  local copies, waits for them, and re-layouts  92.5 us (11%)
  other arithmetic  30.1 us (3%)
  starting transfers between devices  26 us (3%)
  between operations  13.5 us (2%)
    psum x1, waiting for transfers between devices, on_device(): lax.psum((table_coords, table_weights), ('grp', 'dev'))  310 us
    all_gather x1, waiting for transfers between devices, on_device(): total = jnp.sum(lax.all_gather(contribution, 'grp'), axis=0)  148 us
    dot_general x4, matrix products, kernel_sum(): return jnp.einsum('tjs,jsw->tw', kernel, values, precision=high)  86.1 us
    all_to_all x1, waiting for transfers between devices, on_device(): lax.all_to_all(coords, 'dev', split_axis=0, concat_axis=0, tiled=True)  80.8 us
    dot_general x4, matrix products, kernel_sum(): inner = jnp.einsum('dt,jds->tjs', target, sources, precision=high)  64.7 us
    gather x4, local copies, waits for them, and re-layouts, near_leaf(): jnp.take(flat_values, leaf_slots, axis=0)  34 us
  transfers between devices with their start and end apart: 5, of which 4 were waited for; matrix products, arithmetic and copies ran while one was open for 4% of the time, Pallas kernels for 0%

profile of v1, /device:TPU:1, one launch (start us, length us, event | category | flops | bytes accessed | tf_op | source)
XLA Modules:
  0.0 867.0 jit_solution(5999367234654284259)
XLA Ops:
  6.5 0.8 fusion.82
  7.4 0.7 copy.36
  8.1 9.4 %all-to-all-start = ((s32[32,1,2]{2,1,0:T(1,128)}), s32[32,1,2]{2,1,0:T(1,128)S(1)}, u32[]{:S(2)}, u32[]{:S(2)}) async-start(s32[32,1,2]{2,1,0:T(1,128)} %copy.36), calls=%async_computation | async-start | bytes 32768 | tf_op jit(solution)/shard_map/all_to_all | solution.py:33
  17.5 2.7 copy.64
  20.2 4.2 all-to-all-done
  24.4 0.1 copy.37
  24.5 0.1 copy.40
  24.6 0.1 reshape.285
  24.7 0.1 copy.38
  24.8 5.7 gather_fusion.4
  30.6 8.5 broadcast_select_fusion.1
  39.1 5.2 all-to-all-start.1
  44.3 7.4 gather_fusion.5
  51.6 11.6 %broadcast_select_fusion = f32[32,2,512,128]{3,2,1,0:T(8,128)} fusion(f32[32,2,512,128]{3,2,1,0:T(8,128)} %bitcast.102, pred[32,2]{1,0:T(8,128)(4,1)S(1)} %copy.38), kind=kLoop, calls=%fused_computation.86 | loop fusion | flops 4194304 | bytes 33554496 | tf_op jit(solution)/shard_map/jit(_take)/select_n | solution.py:35
  63.2 80.8 %all-to-all-done.1 = f32[32,2,64,512]{3,2,1,0:T(8,128)} async-done(((f32[32,2,64,512]{3,2,1,0:T(8,128)}), f32[32,2,64,512]{3,2,1,0:T(8,128)}, u32[]{:S(2)}, u32[]{:S(2)}) %all-to-all-start.1) | async-done | bytes 8388640 | tf_op jit(solution)/shard_map/all_to_all | solution.py:36
  144.0 11.3 %all-to-all-start.2 = ((f32[32,2,512,128]{3,2,1,0:T(8,128)}), f32[32,2,512,128]{3,2,1,0:T(8,128)}, u32[]{:S(2)}, u32[]{:S(2)}) async-start(f32[32,2,512,128]{3,2,1,0:T(8,128)} %broadcast_select_fusion), calls=%async_computation.2 | async-start | bytes 33554432 | tf_op jit(solution)/shard_map/all_to_all | solution.py:37
  155.3 0.0 all-reduce.3.cloned.1.call-start
  155.4 3.3 copy.43
  158.6 2.6 gather_fusion.6
  161.3 0.1 copy.44
  161.3 2.4 broadcast_in_dim.110
  163.8 3.5 fusion.75
  167.2 1.6 broadcast_in_dim.107
  168.8 0.6 fusion.80
  169.4 0.0 all-reduce.3.cloned.1.call-update
  169.5 0.0 all-gather.3.cloned.1.call-start
  169.5 1.9 reshape.193
  171.4 310.3 %all-reduce.3.cloned.1.call-done = (f32[32,64,256]{2,1,0:T(8,128)}, f32[32,256,128]{2,1,0:T(8,128)}) async-done(((f32[32,64,256]{2,1,0:T(8,128)}, f32[32,256,128]{2,1,0:T(8,128)}), (f32[32,64,256]{2,1,0:T(8,128)}, f32[32,256,128]{2,1,0:T(8,128)})) %all-reduce.3.cloned.1.call-update) | async-done | bytes 6291472 | tf_op jit(solution)/shard_map/psum | solution.py:59
  481.8 223.2 %conditional.1 = (f32[12,512,128]{2,1,0:T(8,128)}) conditional(s32[]{:T(128)} %convert_element_type.3, (s32[]{:T(128)}, s32[12,16]{1,0:T(8,128)}, f32[32,2,64,512]{3,2,1,0:T(8,128)}, f32[32,2,512,128]{3,2,1,0:T(8,128)}, f32[64,12,512]{2,1,0:T(8,128)}) %tuple.20, (f32[64,12,512]{2,1,0:T(8,128)}, s32[12,8]{0,1:T(8,128)S(1)}, f32[32,64,256]{2,1,0:T(8,128)}, ...), branch_computations={%region_2.0_spmd, %region_7.13_spmd} | conditional | flops 9687917568 | bytes 60630836 | solution.py:91
  481.8 0.7 constant_dynamic-slice_fusion.2
  482.4 218.3 %while.19 = (s32[]{:T(128)}, f32[4,512,128]{2,1,0:T(8,128)}, s32[4]{0:T(128)S(1)}, f32[64,12,512]{2,1,0:T(8,128)}, s32[4,16]{1,0:T(4,128)S(1)}, /*index=5*/f32[6...) while((s32[]{:T(128)}, f32[4,512,128]{2,1,0:T(8,128)}, ...), condition=%wide.region_6.7_spmd, body=%wide.region_3.6_spmd.sunk | while | flops 9687917568 | bytes 55387260 | solution.py:74
  482.5 0.6 dynamic_slice.65
  484.9 1.3 constant_dynamic-slice_fusion.9
  486.3 4.1 gather_fusion.3
  490.4 16.2 %fusion.112 = f32[512,16,512]{2,0,1:T(8,128)} fusion(f32[16,64,512]{2,1,0:T(8,128)S(1)} %gather_fusion.3, pred[16]{0:T(512)(128)(4,1)S(1)} %compare_and_fusion.7, f32[64,1,512]{2,1,0:T(1,128)S(1)} %constant_dynamic-slice_fusion.9, pred[]{:T(512)S(6)} %and.57), kind=kOutput, calls=%fused_computation.22.clone.1 | convolution fusion | flops 3221782528 | bytes 19005456 | tf_op jit(solution)/shard_map/cond/branch_0_fun/while/body/eval_jaxpr/dt,jds->tjs/dot_general | solution.py:9
  506.6 0.4 multiply_reduce_fusion.5
  507.0 8.5 gather_fusion.2
  515.5 21.5 %fusion.114 = f32[4,512,128]{2,1,0:T(8,128)} fusion(f32[4,512,128]{2,1,0:T(8,128)} %get-tuple-element.314, s32[]{:T(128)} %get-tuple-element.313, f32[16,512,128]{2,1,0:T(8,128)} %gather_fusion.2, pred[16]{0:T(512)(128)(4,1)S(1)} %compare_and_fusion.7, f32[512,16,512]{2,0,1:T(8,128)} %fusion.112, f32[16,512]{1,0:T(8,128)S(1)} %multiply_reduce_fusion.5, ...), kind=kOutput, calls=%fused_computation.25.clone.1 | convolution fusion | flops 6464471040 | bytes 21269008 | tf_op jit(solution)/shard_map/cond/branch_0_fun/while/body/eval_jaxpr/tjs,jsw->tw/dot_general | solution.py:14
  537.0 0.6 dynamic_slice.65
  539.5 1.3 constant_dynamic-slice_fusion.9
  540.9 4.1 gather_fusion.3
  545.0 16.2 %fusion.112 = f32[512,16,512]{2,0,1:T(8,128)} fusion(f32[16,64,512]{2,1,0:T(8,128)S(1)} %gather_fusion.3, pred[16]{0:T(512)(128)(4,1)S(1)} %compare_and_fusion.7, f32[64,1,512]{2,1,0:T(1,128)S(1)} %constant_dynamic-slice_fusion.9, pred[]{:T(512)S(6)} %and.57), kind=kOutput, calls=%fused_computation.22.clone.1 | convolution fusion | flops 3221782528 | bytes 19005456 | tf_op jit(solution)/shard_map/cond/branch_0_fun/while/body/eval_jaxpr/dt,jds->tjs/dot_general | solution.py:9
  561.2 0.4 multiply_reduce_fusion.5
  561.5 8.5 gather_fusion.2
  570.1 21.5 %fusion.114 = f32[4,512,128]{2,1,0:T(8,128)} fusion(f32[4,512,128]{2,1,0:T(8,128)} %get-tuple-element.314, s32[]{:T(128)} %get-tuple-element.313, f32[16,512,128]{2,1,0:T(8,128)} %gather_fusion.2, pred[16]{0:T(512)(128)(4,1)S(1)} %compare_and_fusion.7, f32[512,16,512]{2,0,1:T(8,128)} %fusion.112, f32[16,512]{1,0:T(8,128)S(1)} %multiply_reduce_fusion.5, ...), kind=kOutput, calls=%fused_computation.25.clone.1 | convolution fusion | flops 6464471040 | bytes 21269008 | tf_op jit(solution)/shard_map/cond/branch_0_fun/while/body/eval_jaxpr/tjs,jsw->tw/dot_general | solution.py:14
  591.6 0.6 dynamic_slice.65
  594.1 1.3 constant_dynamic-slice_fusion.9
  595.4 4.1 gather_fusion.3
  599.5 16.2 %fusion.112 = f32[512,16,512]{2,0,1:T(8,128)} fusion(f32[16,64,512]{2,1,0:T(8,128)S(1)} %gather_fusion.3, pred[16]{0:T(512)(128)(4,1)S(1)} %compare_and_fusion.7, f32[64,1,512]{2,1,0:T(1,128)S(1)} %constant_dynamic-slice_fusion.9, pred[]{:T(512)S(6)} %and.57), kind=kOutput, calls=%fused_computation.22.clone.1 | convolution fusion | flops 3221782528 | bytes 19005456 | tf_op jit(solution)/shard_map/cond/branch_0_fun/while/body/eval_jaxpr/dt,jds->tjs/dot_general | solution.py:9
  615.7 0.4 multiply_reduce_fusion.5
  616.1 8.5 gather_fusion.2
  624.6 21.5 %fusion.114 = f32[4,512,128]{2,1,0:T(8,128)} fusion(f32[4,512,128]{2,1,0:T(8,128)} %get-tuple-element.314, s32[]{:T(128)} %get-tuple-element.313, f32[16,512,128]{2,1,0:T(8,128)} %gather_fusion.2, pred[16]{0:T(512)(128)(4,1)S(1)} %compare_and_fusion.7, f32[512,16,512]{2,0,1:T(8,128)} %fusion.112, f32[16,512]{1,0:T(8,128)S(1)} %multiply_reduce_fusion.5, ...), kind=kOutput, calls=%fused_computation.25.clone.1 | convolution fusion | flops 6464471040 | bytes 21269008 | tf_op jit(solution)/shard_map/cond/branch_0_fun/while/body/eval_jaxpr/tjs,jsw->tw/dot_general | solution.py:14
  646.2 0.6 dynamic_slice.65
  648.6 1.3 constant_dynamic-slice_fusion.9
  650.0 4.1 gather_fusion.3
  654.1 16.2 %fusion.112 = f32[512,16,512]{2,0,1:T(8,128)} fusion(f32[16,64,512]{2,1,0:T(8,128)S(1)} %gather_fusion.3, pred[16]{0:T(512)(128)(4,1)S(1)} %compare_and_fusion.7, f32[64,1,512]{2,1,0:T(1,128)S(1)} %constant_dynamic-slice_fusion.9, pred[]{:T(512)S(6)} %and.57), kind=kOutput, calls=%fused_computation.22.clone.1 | convolution fusion | flops 3221782528 | bytes 19005456 | tf_op jit(solution)/shard_map/cond/branch_0_fun/while/body/eval_jaxpr/dt,jds->tjs/dot_general | solution.py:9
  670.3 0.4 multiply_reduce_fusion.5
  670.7 8.5 gather_fusion.2
  679.2 21.5 %fusion.114 = f32[4,512,128]{2,1,0:T(8,128)} fusion(f32[4,512,128]{2,1,0:T(8,128)} %get-tuple-element.314, s32[]{:T(128)} %get-tuple-element.313, f32[16,512,128]{2,1,0:T(8,128)} %gather_fusion.2, pred[16]{0:T(512)(128)(4,1)S(1)} %compare_and_fusion.7, f32[512,16,512]{2,0,1:T(8,128)} %fusion.112, f32[16,512]{1,0:T(8,128)S(1)} %multiply_reduce_fusion.5, ...), kind=kOutput, calls=%fused_computation.25.clone.1 | convolution fusion | flops 6464471040 | bytes 21269008 | tf_op jit(solution)/shard_map/cond/branch_0_fun/while/body/eval_jaxpr/tjs,jsw->tw/dot_general | solution.py:14
  700.7 2.0 broadcast.190
  702.7 2.3 constant_dynamic-update-slice_fusion
  705.0 0.0 all-gather.3.cloned.1.call-update
  705.0 147.6 %all-gather.3.cloned.1.call-done = f32[48,512,128]{2,1,0:T(8,128)} async-done(((f32[12,512,128]{2,1,0:T(8,128)}), f32[48,512,128]{2,1,0:T(8,128)}) %all-gather.3.cloned.1.call-update) | async-done | bytes 12582928 | tf_op jit(solution)/shard_map/all_gather | solution.py:92
  852.6 7.6 reduce_sum.45
  (35 shorter events, 0.3 us)
Async XLA Ops:
  6.5 37.7 %copy-start = (f32[6144,128]{1,0:T(8,128)S(1)}, f32[6144,128]{1,0:T(8,128)}, u32[]{:S(2)}) copy-start(f32[6144,128]{1,0:T(8,128)} %param.16) | copy-start | bytes 9437188
  8.1 16.4 %all-to-all-start = ((s32[32,1,2]{2,1,0:T(1,128)}), s32[32,1,2]{2,1,0:T(1,128)S(1)}, u32[]{:S(2)}, u32[]{:S(2)}) async-start(s32[32,1,2]{2,1,0:T(1,128)} %copy.36), calls=%async_computation | async-start | bytes 32768 | tf_op jit(solution)/shard_map/all_to_all | solution.py:33
  39.1 105.0 %all-to-all-start.1 = ((f32[32,2,64,512]{3,2,1,0:T(8,128)}), f32[32,2,64,512]{3,2,1,0:T(8,128)}, u32[]{:S(2)}, u32[]{:S(2)}) async-start(f32[32,2,64,512]{3,2,1,0:T(8,128)} %broadcast_select_fusion.1), calls=%async_computation.1 | async-start | bytes 16777216 | tf_op jit(solution)/shard_map/all_to_all | solution.py:36
  144.0 337.7 %all-to-all-start.2 = ((f32[32,2,512,128]{3,2,1,0:T(8,128)}), f32[32,2,512,128]{3,2,1,0:T(8,128)}, u32[]{:S(2)}, u32[]{:S(2)}) async-start(f32[32,2,512,128]{3,2,1,0:T(8,128)} %broadcast_select_fusion), calls=%async_computation.2 | async-start | bytes 33554432 | tf_op jit(solution)/shard_map/all_to_all | solution.py:37
  155.3 3.3 copy-start.4
  155.3 326.4 %all-reduce.3.cloned.1.call-start = ((), (), s32[]{:S(2)}) async-start(), calls=%async_computation.4 | async-start | bytes 12582912 | tf_op jit(solution)/shard_map/psum | solution.py:59
  167.2 2.3 copy-start.2
  169.4 312.3 %copy-start.3 = (s32[12,8]{0,1:T(8,128)S(1)}, s32[12,8]{0,1:T(8,128)}, u32[]{:S(2)}) copy-start(s32[12,8]{0,1:T(8,128)} %param.20) | copy-start | bytes 1156
  169.5 683.1 %all-gather.3.cloned.1.call-start = ((), (), s32[]{:S(2)}) async-start(), calls=%async_computation.3 | async-start | bytes 15728640 | tf_op jit(solution)/shard_map/all_gather | solution.py:92
  852.6 7.6 copy-start.1
Sparse Core Ops, SparseCore 0:
  169.6 312.1 all-reduce.2
  705.1 147.4 all-gather.2
